TPU v7x, 32 devices: a whole 2x2x4 slice. The times are simulated.
32 devices in a mesh: slab: 8 (over z, y), face: 4 (over x, core).
Axes of the slice: x: 2, y: 2, z: 4, core: 2. Of those that a mesh axis runs over, the one named last changes fastest.
Arguments:
- rhs: float32 [8, 16, 6, 128], P('slab', 'face'), may hold values from -6 to 6
- iterate: float32 [8, 16, 6, 128], P('slab', 'face'), may hold values from -6 to 6
- op_self: float32 [8, 16, 128, 128], P('slab', 'face'), may hold values from -0.5 to 0.5
- op_couple: float32 [8, 16, 4, 128, 128], P('slab', 'face'), may hold values from -0.25 to 0.25
- fill_slot: int32 [8, 16, 6], P('slab', 'face'), may hold values from 0 to 31
- fill_count: int32 [8, 16], P('slab', 'face'), may hold values from 1 to 6
- fill_blocks: float32 [8, 16, 6, 128, 128], P('slab', 'face'), may hold values from -1.25 to 1.25
- diag_inverse: float32 [8, 16, 128, 128], P('slab', 'face'), may hold values from -1.25 to 1.25
Outputs:
- solution: float32 [8, 16, 6, 128], P('slab', 'face')
- image: float32 [8, 16, 6, 128], P('slab', 'face')
All inputs are finite; a program needn't handle non-finite values.
Results may differ from a plain program's by a relative error of at most 0.0003.
Values sent between devices are 32-bit elements; how exact they have to be, the bound alone decides.
A program may use at most 64 MiB of HBM per device.

v0:
```python
import jax
import jax.numpy as jnp
from jax import lax
from jax.sharding import PartitionSpec as P

BLK = 128
LOADS = 6
K_FILL = 6
REACH = 2


def padded_2(block, sides, width):
    for axis, dim in sides:
        count = lax.axis_size(axis)
        forward = [(i, i + 1) for i in range(count - 1)]
        backward = [(target, source) for source, target in forward]
        low = lax.ppermute(
            lax.slice_in_dim(block, block.shape[dim] - width, None, axis=dim), axis, forward
        )
        high = lax.ppermute(lax.slice_in_dim(block, 0, width, axis=dim), axis, backward)
        block = jnp.concatenate([low, block, high], axis=dim)
    return block


def passed_along(block, axis, distance):
    devices = range(lax.axis_size(axis))
    route = [(i - distance, i) for i in devices if i - distance in devices]
    return lax.ppermute(block, axis, route)


def apply_blocks(mats, vecs):
    return jnp.einsum("srij,srlj->srli", mats, vecs, precision=lax.Precision.HIGHEST)


def operator(field, op_self, op_couple):
    padded = padded_2(field, (("slab", 0), ("face", 1)), 1)
    out = apply_blocks(op_self, field)
    out = out + apply_blocks(op_couple[:, :, 0], padded[:-2, 1:-1])
    out = out + apply_blocks(op_couple[:, :, 1], padded[2:, 1:-1])
    out = out + apply_blocks(op_couple[:, :, 2], padded[1:-1, :-2])
    out = out + apply_blocks(op_couple[:, :, 3], padded[1:-1, 2:])
    return out


def fill_term(source, lower, slots, used, blocks):
    span = source.shape[0]
    local = slots - lower
    inside = ((local >= 0) & (local < span)).astype(jnp.float32) * used
    picked = source[jnp.clip(local, 0, span - 1)]
    return jnp.einsum(
        "rkij,rklj->rli", blocks, picked * inside[:, :, None, None], precision=lax.Precision.HIGHEST
    )


def body(rhs, iterate, op_self, op_couple, fill_slot, fill_count, fill_blocks, diag_inverse):
    residual = (rhs - operator(iterate, op_self, op_couple))[0]
    slots = fill_slot[0]
    blocks = fill_blocks[0]
    inverse = diag_inverse[0]
    used = (jnp.arange(K_FILL, dtype=jnp.int32)[None, :] < fill_count[0][:, None]).astype(
        jnp.float32
    )
    rows_local = residual.shape[0]
    rows_slab = rows_local * lax.axis_size("face")
    steps = lax.axis_size("slab")
    mine = lax.axis_index("slab")
    start_sol = jnp.zeros_like(residual)

    def advance(step, carry):
        window, result = carry
        acc = fill_term(window, 0, slots, used, blocks)
        solved = jnp.einsum(
            "rij,rlj->rli", inverse, residual - acc, precision=lax.Precision.HIGHEST
        )
        result = jnp.where(mine == step, solved, result)
        whole = lax.all_gather(solved, "face", axis=0, tiled=True)
        window = passed_along(jnp.concatenate([window[rows_slab:], whole], axis=0), "slab", 1)
        return (window, result)

    start_win = jnp.zeros((REACH * rows_slab, LOADS, BLK), jnp.float32)
    _, result = lax.fori_loop(0, steps, advance, (start_win, start_sol))
    solution = result[None]
    image = operator(solution, op_self, op_couple)
    return (solution, image)


def solution(mesh):
    return jax.shard_map(
        body,
        mesh=mesh,
        in_specs=(
            P("slab", "face", None, None),
            P("slab", "face", None, None),
            P("slab", "face", None, None),
            P("slab", "face", None, None, None),
            P("slab", "face", None),
            P("slab", "face"),
            P("slab", "face", None, None, None),
            P("slab", "face", None, None),
        ),
        out_specs=(P("slab", "face", None, None), P("slab", "face", None, None)),
        check_vma=False,
    )
```

profile of v0, /device:TPU:5, one launch (start us, length us, event | category | flops | bytes accessed | tf_op | source)
XLA Modules:
  0.0 181.5 jit_solution(4526185078878282599)
XLA Ops:
  1.5 3.1 %collective-permute-start.1 = (f32[1,4,6,128]{3,2,1,0:T(8,128)S(1)}, f32[1,4,6,128]{3,2,1,0:T(8,128)S(1)}, u32[]{:S(2)}, u32[]{:S(2)}) collective-permute-start(f32[1,4,6,128]{3,2,1,0:T(8,128)S(1)} %copy.22), channel_id=1, source_target_pairs={{0,4},{4,8},{8,12},{12,16},{16,20},{20,24},{24,28},{1,5},{5,9},{9,... | collective-permute-start | bytes 36872 | tf_op jit(solution)/shard_map/ppermute | solution.py:17
  4.7 2.1 %collective-permute-start.2 = (f32[1,4,6,128]{3,2,1,0:T(8,128)S(1)}, f32[1,4,6,128]{3,2,1,0:T(8,128)S(1)}, u32[]{:S(2)}, u32[]{:S(2)}) collective-permute-start(f32[1,4,6,128]{3,2,1,0:T(8,128)S(1)} %copy.22), channel_id=1, source_target_pairs={{4,0},{8,4},{12,8},{16,12},{20,16},{24,20},{28,24},{5,1},{9,5},{13... | collective-permute-start | bytes 36872 | tf_op jit(solution)/shard_map/ppermute | solution.py:20
  8.8 1.3 collective-permute-done.2
  10.1 5.1 %collective-permute-start.3 = (f32[3,1,6,128]{3,2,1,0:T(8,128)S(1)}, f32[3,1,6,128]{3,2,1,0:T(8,128)S(1)}, u32[]{:S(2)}, u32[]{:S(2)}) collective-permute-start(f32[3,1,6,128]{3,2,1,0:T(8,128)S(1)} %get-tuple-element.216), channel_id=1, source_target_pairs={{0,1},{1,2},{2,3},{4,5},{5,6},{6,7},{8,9},{9,10},{10,11},{12,13},{... | collective-permute-start | bytes 27656 | tf_op jit(solution)/shard_map/ppermute | solution.py:17
  15.2 1.9 %collective-permute-start.4 = (f32[3,1,6,128]{3,2,1,0:T(8,128)S(1)}, f32[3,1,6,128]{3,2,1,0:T(8,128)S(1)}, u32[]{:S(2)}, u32[]{:S(2)}) collective-permute-start(f32[3,1,6,128]{3,2,1,0:T(8,128)S(1)} %get-tuple-element.217), channel_id=1, source_target_pairs={{1,0},{2,1},{3,2},{5,4},{6,5},{7,6},{9,8},{10,9},{11,10},{13,12},{... | collective-permute-start | bytes 27656 | tf_op jit(solution)/shard_map/ppermute | solution.py:20
  17.1 1.5 convolution_add_fusion.3
  18.6 1.5 fusion.19
  20.2 1.5 fusion.15
  21.6 1.5 fusion.12
  23.2 135.3 %while.16 = (s32[]{:T(128)}, f32[32,6,128]{2,1,0:T(8,128)S(1)}, f32[4,6,128]{2,1,0:T(8,128)S(1)}, s32[4,6]{1,0:T(4,128)S(1)}, f32[4,6,128,128]{3,2,1,0:T(8,128)S...) while((s32[]{:T(128)}, f32[32,6,128]{2,1,0:T(8,128)S(1)}, ...), condition=%wide.region_1.2_spmd.clone, body=%wide.region_0.1_spmd.clone.sunk | while | flops 33083636 | bytes 2884633 | solution.py:81
  24.0 1.4 fusion.72
  25.9 5.1 %all_gather.9 = f32[16,6,128]{2,1,0:T(8,128)S(1)} all-gather(f32[4,6,128]{2,1,0:T(8,128)S(1)} %get-tuple-element.275), channel_id=1, replica_groups=mesh['slab'=8,'face'=4] {'face'}, dimensions={0}, use_global_device_ids=true | all-gather | bytes 61440 | tf_op jit(solution)/shard_map/while/body/eval_jaxpr/all_gather | solution.py:76
  31.7 2.2 %collective-permute-start = (f32[32,6,128]{2,1,0:T(8,128)}, f32[32,6,128]{2,1,0:T(8,128)S(1)}, u32[]{:S(2)}, u32[]{:S(2)}) collective-permute-start(f32[32,6,128]{2,1,0:T(8,128)} %pad_maximum_fusion.17), channel_id=1, source_target_pairs={{0,4},{4,8},{8,12},{12,16},{16,20},{20,24},{24,28},{1,5},{5,9},{9,... | collective-permute-start | bytes 294920 | tf_op jit(solution)/shard_map/while/body/eval_jaxpr/ppermute | solution.py:28
  33.9 4.8 %collective-permute-done = f32[32,6,128]{2,1,0:T(8,128)S(1)} collective-permute-done((f32[32,6,128]{2,1,0:T(8,128)}, f32[32,6,128]{2,1,0:T(8,128)S(1)}, u32[]{:S(2)}, u32[]{:S(2)}) %collective-permute-start) | collective-permute-done | bytes 98336 | tf_op jit(solution)/shard_map/while/body/eval_jaxpr/ppermute | solution.py:28
  39.5 1.4 fusion.72
  41.4 6.0 %all_gather.9 = f32[16,6,128]{2,1,0:T(8,128)S(1)} all-gather(f32[4,6,128]{2,1,0:T(8,128)S(1)} %get-tuple-element.275), channel_id=1, replica_groups=mesh['slab'=8,'face'=4] {'face'}, dimensions={0}, use_global_device_ids=true | all-gather | bytes 61440 | tf_op jit(solution)/shard_map/while/body/eval_jaxpr/all_gather | solution.py:76
  48.1 3.1 %collective-permute-start = (f32[32,6,128]{2,1,0:T(8,128)}, f32[32,6,128]{2,1,0:T(8,128)S(1)}, u32[]{:S(2)}, u32[]{:S(2)}) collective-permute-start(f32[32,6,128]{2,1,0:T(8,128)} %pad_maximum_fusion.17), channel_id=1, source_target_pairs={{0,4},{4,8},{8,12},{12,16},{16,20},{20,24},{24,28},{1,5},{5,9},{9,... | collective-permute-start | bytes 294920 | tf_op jit(solution)/shard_map/while/body/eval_jaxpr/ppermute | solution.py:28
  51.3 3.9 %collective-permute-done = f32[32,6,128]{2,1,0:T(8,128)S(1)} collective-permute-done((f32[32,6,128]{2,1,0:T(8,128)}, f32[32,6,128]{2,1,0:T(8,128)S(1)}, u32[]{:S(2)}, u32[]{:S(2)}) %collective-permute-start) | collective-permute-done | bytes 98336 | tf_op jit(solution)/shard_map/while/body/eval_jaxpr/ppermute | solution.py:28
  55.9 1.4 fusion.72
  57.9 6.0 %all_gather.9 = f32[16,6,128]{2,1,0:T(8,128)S(1)} all-gather(f32[4,6,128]{2,1,0:T(8,128)S(1)} %get-tuple-element.275), channel_id=1, replica_groups=mesh['slab'=8,'face'=4] {'face'}, dimensions={0}, use_global_device_ids=true | all-gather | bytes 61440 | tf_op jit(solution)/shard_map/while/body/eval_jaxpr/all_gather | solution.py:76
  64.6 4.0 %collective-permute-start = (f32[32,6,128]{2,1,0:T(8,128)}, f32[32,6,128]{2,1,0:T(8,128)S(1)}, u32[]{:S(2)}, u32[]{:S(2)}) collective-permute-start(f32[32,6,128]{2,1,0:T(8,128)} %pad_maximum_fusion.17), channel_id=1, source_target_pairs={{0,4},{4,8},{8,12},{12,16},{16,20},{20,24},{24,28},{1,5},{5,9},{9,... | collective-permute-start | bytes 294920 | tf_op jit(solution)/shard_map/while/body/eval_jaxpr/ppermute | solution.py:28
  68.7 3.0 %collective-permute-done = f32[32,6,128]{2,1,0:T(8,128)S(1)} collective-permute-done((f32[32,6,128]{2,1,0:T(8,128)}, f32[32,6,128]{2,1,0:T(8,128)S(1)}, u32[]{:S(2)}, u32[]{:S(2)}) %collective-permute-start) | collective-permute-done | bytes 98336 | tf_op jit(solution)/shard_map/while/body/eval_jaxpr/ppermute | solution.py:28
  72.5 1.4 fusion.72
  74.4 6.0 %all_gather.9 = f32[16,6,128]{2,1,0:T(8,128)S(1)} all-gather(f32[4,6,128]{2,1,0:T(8,128)S(1)} %get-tuple-element.275), channel_id=1, replica_groups=mesh['slab'=8,'face'=4] {'face'}, dimensions={0}, use_global_device_ids=true | all-gather | bytes 61440 | tf_op jit(solution)/shard_map/while/body/eval_jaxpr/all_gather | solution.py:76
  81.1 4.9 %collective-permute-start = (f32[32,6,128]{2,1,0:T(8,128)}, f32[32,6,128]{2,1,0:T(8,128)S(1)}, u32[]{:S(2)}, u32[]{:S(2)}) collective-permute-start(f32[32,6,128]{2,1,0:T(8,128)} %pad_maximum_fusion.17), channel_id=1, source_target_pairs={{0,4},{4,8},{8,12},{12,16},{16,20},{20,24},{24,28},{1,5},{5,9},{9,... | collective-permute-start | bytes 294920 | tf_op jit(solution)/shard_map/while/body/eval_jaxpr/ppermute | solution.py:28
  86.0 3.0 %collective-permute-done = f32[32,6,128]{2,1,0:T(8,128)S(1)} collective-permute-done((f32[32,6,128]{2,1,0:T(8,128)}, f32[32,6,128]{2,1,0:T(8,128)S(1)}, u32[]{:S(2)}, u32[]{:S(2)}) %collective-permute-start) | collective-permute-done | bytes 98336 | tf_op jit(solution)/shard_map/while/body/eval_jaxpr/ppermute | solution.py:28
  89.8 1.4 fusion.72
  91.8 6.0 %all_gather.9 = f32[16,6,128]{2,1,0:T(8,128)S(1)} all-gather(f32[4,6,128]{2,1,0:T(8,128)S(1)} %get-tuple-element.275), channel_id=1, replica_groups=mesh['slab'=8,'face'=4] {'face'}, dimensions={0}, use_global_device_ids=true | all-gather | bytes 61440 | tf_op jit(solution)/shard_map/while/body/eval_jaxpr/all_gather | solution.py:76
  98.5 4.9 %collective-permute-start = (f32[32,6,128]{2,1,0:T(8,128)}, f32[32,6,128]{2,1,0:T(8,128)S(1)}, u32[]{:S(2)}, u32[]{:S(2)}) collective-permute-start(f32[32,6,128]{2,1,0:T(8,128)} %pad_maximum_fusion.17), channel_id=1, source_target_pairs={{0,4},{4,8},{8,12},{12,16},{16,20},{20,24},{24,28},{1,5},{5,9},{9,... | collective-permute-start | bytes 294920 | tf_op jit(solution)/shard_map/while/body/eval_jaxpr/ppermute | solution.py:28
  103.4 3.0 %collective-permute-done = f32[32,6,128]{2,1,0:T(8,128)S(1)} collective-permute-done((f32[32,6,128]{2,1,0:T(8,128)}, f32[32,6,128]{2,1,0:T(8,128)S(1)}, u32[]{:S(2)}, u32[]{:S(2)}) %collective-permute-start) | collective-permute-done | bytes 98336 | tf_op jit(solution)/shard_map/while/body/eval_jaxpr/ppermute | solution.py:28
  107.2 1.4 fusion.72
  109.2 6.0 %all_gather.9 = f32[16,6,128]{2,1,0:T(8,128)S(1)} all-gather(f32[4,6,128]{2,1,0:T(8,128)S(1)} %get-tuple-element.275), channel_id=1, replica_groups=mesh['slab'=8,'face'=4] {'face'}, dimensions={0}, use_global_device_ids=true | all-gather | bytes 61440 | tf_op jit(solution)/shard_map/while/body/eval_jaxpr/all_gather | solution.py:76
  115.9 4.9 %collective-permute-start = (f32[32,6,128]{2,1,0:T(8,128)}, f32[32,6,128]{2,1,0:T(8,128)S(1)}, u32[]{:S(2)}, u32[]{:S(2)}) collective-permute-start(f32[32,6,128]{2,1,0:T(8,128)} %pad_maximum_fusion.17), channel_id=1, source_target_pairs={{0,4},{4,8},{8,12},{12,16},{16,20},{20,24},{24,28},{1,5},{5,9},{9,... | collective-permute-start | bytes 294920 | tf_op jit(solution)/shard_map/while/body/eval_jaxpr/ppermute | solution.py:28
  120.8 3.0 %collective-permute-done = f32[32,6,128]{2,1,0:T(8,128)S(1)} collective-permute-done((f32[32,6,128]{2,1,0:T(8,128)}, f32[32,6,128]{2,1,0:T(8,128)S(1)}, u32[]{:S(2)}, u32[]{:S(2)}) %collective-permute-start) | collective-permute-done | bytes 98336 | tf_op jit(solution)/shard_map/while/body/eval_jaxpr/ppermute | solution.py:28
  124.6 1.4 fusion.72
  126.5 6.0 %all_gather.9 = f32[16,6,128]{2,1,0:T(8,128)S(1)} all-gather(f32[4,6,128]{2,1,0:T(8,128)S(1)} %get-tuple-element.275), channel_id=1, replica_groups=mesh['slab'=8,'face'=4] {'face'}, dimensions={0}, use_global_device_ids=true | all-gather | bytes 61440 | tf_op jit(solution)/shard_map/while/body/eval_jaxpr/all_gather | solution.py:76
  133.3 4.9 %collective-permute-start = (f32[32,6,128]{2,1,0:T(8,128)}, f32[32,6,128]{2,1,0:T(8,128)S(1)}, u32[]{:S(2)}, u32[]{:S(2)}) collective-permute-start(f32[32,6,128]{2,1,0:T(8,128)} %pad_maximum_fusion.17), channel_id=1, source_target_pairs={{0,4},{4,8},{8,12},{12,16},{16,20},{20,24},{24,28},{1,5},{5,9},{9,... | collective-permute-start | bytes 294920 | tf_op jit(solution)/shard_map/while/body/eval_jaxpr/ppermute | solution.py:28
  138.2 3.0 %collective-permute-done = f32[32,6,128]{2,1,0:T(8,128)S(1)} collective-permute-done((f32[32,6,128]{2,1,0:T(8,128)}, f32[32,6,128]{2,1,0:T(8,128)S(1)}, u32[]{:S(2)}, u32[]{:S(2)}) %collective-permute-start) | collective-permute-done | bytes 98336 | tf_op jit(solution)/shard_map/while/body/eval_jaxpr/ppermute | solution.py:28
  142.0 1.4 fusion.72
  143.9 6.0 %all_gather.9 = f32[16,6,128]{2,1,0:T(8,128)S(1)} all-gather(f32[4,6,128]{2,1,0:T(8,128)S(1)} %get-tuple-element.275), channel_id=1, replica_groups=mesh['slab'=8,'face'=4] {'face'}, dimensions={0}, use_global_device_ids=true | all-gather | bytes 61440 | tf_op jit(solution)/shard_map/while/body/eval_jaxpr/all_gather | solution.py:76
  150.6 4.9 %collective-permute-start = (f32[32,6,128]{2,1,0:T(8,128)}, f32[32,6,128]{2,1,0:T(8,128)S(1)}, u32[]{:S(2)}, u32[]{:S(2)}) collective-permute-start(f32[32,6,128]{2,1,0:T(8,128)} %pad_maximum_fusion.17), channel_id=1, source_target_pairs={{0,4},{4,8},{8,12},{12,16},{16,20},{20,24},{24,28},{1,5},{5,9},{9,... | collective-permute-start | bytes 294920 | tf_op jit(solution)/shard_map/while/body/eval_jaxpr/ppermute | solution.py:28
  155.5 3.0 %collective-permute-done = f32[32,6,128]{2,1,0:T(8,128)S(1)} collective-permute-done((f32[32,6,128]{2,1,0:T(8,128)}, f32[32,6,128]{2,1,0:T(8,128)S(1)}, u32[]{:S(2)}, u32[]{:S(2)}) %collective-permute-start) | collective-permute-done | bytes 98336 | tf_op jit(solution)/shard_map/while/body/eval_jaxpr/ppermute | solution.py:28
  158.6 4.9 %collective-permute-start.5 = (f32[1,4,6,128]{3,2,1,0:T(8,128)S(1)}, f32[1,4,6,128]{3,2,1,0:T(8,128)S(1)}, u32[]{:S(2)}, u32[]{:S(2)}) collective-permute-start(f32[1,4,6,128]{3,2,1,0:T(8,128)S(1)} %bitcast.102), channel_id=1, source_target_pairs={{0,4},{4,8},{8,12},{12,16},{16,20},{20,24},{24,28},{1,5},{5,9},{9,... | collective-permute-start | bytes 36872 | tf_op jit(solution)/shard_map/ppermute | solution.py:17
  163.5 1.9 %collective-permute-start.6 = (f32[1,4,6,128]{3,2,1,0:T(8,128)S(1)}, f32[1,4,6,128]{3,2,1,0:T(8,128)S(1)}, u32[]{:S(2)}, u32[]{:S(2)}) collective-permute-start(f32[1,4,6,128]{3,2,1,0:T(8,128)S(1)} %bitcast.103), channel_id=1, source_target_pairs={{4,0},{8,4},{12,8},{16,12},{20,16},{24,20},{28,24},{5,1},{9,5},{13... | collective-permute-start | bytes 36872 | tf_op jit(solution)/shard_map/ppermute | solution.py:20
  166.5 2.3 %collective-permute-done.6 = f32[1,4,6,128]{3,2,1,0:T(8,128)S(1)} collective-permute-done((f32[1,4,6,128]{3,2,1,0:T(8,128)S(1)}, f32[1,4,6,128]{3,2,1,0:T(8,128)S(1)}, u32[]{:S(2)}, u32[]{:S(2)}) %collective-permute-start.6) | collective-permute-done | bytes 12320 | tf_op jit(solution)/shard_map/ppermute | solution.py:20
  168.8 5.9 %collective-permute-start.7 = (f32[3,1,6,128]{3,2,1,0:T(8,128)S(1)}, f32[3,1,6,128]{3,2,1,0:T(8,128)S(1)}, u32[]{:S(2)}, u32[]{:S(2)}) collective-permute-start(f32[3,1,6,128]{3,2,1,0:T(8,128)S(1)} %get-tuple-element.214), channel_id=1, source_target_pairs={{0,1},{1,2},{2,3},{4,5},{5,6},{6,7},{8,9},{9,10},{10,11},{12,13},{... | collective-permute-start | bytes 27656 | tf_op jit(solution)/shard_map/ppermute | solution.py:17
  174.8 1.9 %collective-permute-start.8 = (f32[3,1,6,128]{3,2,1,0:T(8,128)S(1)}, f32[3,1,6,128]{3,2,1,0:T(8,128)S(1)}, u32[]{:S(2)}, u32[]{:S(2)}) collective-permute-start(f32[3,1,6,128]{3,2,1,0:T(8,128)S(1)} %get-tuple-element.215), channel_id=1, source_target_pairs={{1,0},{2,1},{3,2},{5,4},{6,5},{7,6},{9,8},{10,9},{11,10},{13,12},{... | collective-permute-start | bytes 27656 | tf_op jit(solution)/shard_map/ppermute | solution.py:20
  177.8 2.0 %collective-permute-done.8 = f32[3,1,6,128]{3,2,1,0:T(8,128)S(1)} collective-permute-done((f32[3,1,6,128]{3,2,1,0:T(8,128)S(1)}, f32[3,1,6,128]{3,2,1,0:T(8,128)S(1)}, u32[]{:S(2)}, u32[]{:S(2)}) %collective-permute-start.8) | collective-permute-done | bytes 9248 | tf_op jit(solution)/shard_map/ppermute | solution.py:20
  (97 shorter events, 22.6 us)
Async XLA Ops:
  0.6 6.2 %copy-start = (f32[1,4,128,128]{3,2,1,0:T(8,128)S(1)}, f32[1,4,128,128]{3,2,1,0:T(8,128)}, u32[]{:S(2)}) copy-start(f32[1,4,128,128]{3,2,1,0:T(8,128)} %param.12) | copy-start | bytes 786436
  0.6 22.5 %copy-start.4 = (s32[1,4,6]{2,1,0:T(4,128)S(1)}, s32[1,4,6]{2,1,0:T(4,128)}, u32[]{:S(2)}) copy-start(s32[1,4,6]{2,1,0:T(4,128)} %param.14) | copy-start | bytes 292
  0.7 22.5 %copy-start.1 = (f32[1,4,6,128,128]{4,3,2,1,0:T(8,128)S(1)}, f32[1,4,6,128,128]{4,3,2,1,0:T(8,128)}, u32[]{:S(2)}) copy-start(f32[1,4,6,128,128]{4,3,2,1,0:T(8,128)} %param.16) | copy-start | bytes 4718596
  0.7 22.5 %copy-start.2 = (f32[1,4,128,128]{3,2,1,0:T(8,128)S(1)}, f32[1,4,128,128]{3,2,1,0:T(8,128)}, u32[]{:S(2)}) copy-start(f32[1,4,128,128]{3,2,1,0:T(8,128)} %param.17) | copy-start | bytes 786436
  0.7 22.5 %copy-start.5 = (s32[1,4]{1,0:T(1,128)S(1)}, s32[1,4]{1,0:T(1,128)}, u32[]{:S(2)}) copy-start(s32[1,4]{1,0:T(1,128)} %param.15) | copy-start | bytes 52
  1.5 6.5 %collective-permute-start.1 = (f32[1,4,6,128]{3,2,1,0:T(8,128)S(1)}, f32[1,4,6,128]{3,2,1,0:T(8,128)S(1)}, u32[]{:S(2)}, u32[]{:S(2)}) collective-permute-start(f32[1,4,6,128]{3,2,1,0:T(8,128)S(1)} %copy.22), channel_id=1, source_target_pairs={{0,4},{4,8},{8,12},{12,16},{16,20},{20,24},{24,28},{1,5},{5,9},{9,... | collective-permute-start | bytes 36872 | tf_op jit(solution)/shard_map/ppermute | solution.py:17
  4.7 5.4 %collective-permute-start.2 = (f32[1,4,6,128]{3,2,1,0:T(8,128)S(1)}, f32[1,4,6,128]{3,2,1,0:T(8,128)S(1)}, u32[]{:S(2)}, u32[]{:S(2)}) collective-permute-start(f32[1,4,6,128]{3,2,1,0:T(8,128)S(1)} %copy.22), channel_id=1, source_target_pairs={{4,0},{8,4},{12,8},{16,12},{20,16},{24,20},{28,24},{5,1},{9,5},{13... | collective-permute-start | bytes 36872 | tf_op jit(solution)/shard_map/ppermute | solution.py:20
  10.1 8.5 %collective-permute-start.3 = (f32[3,1,6,128]{3,2,1,0:T(8,128)S(1)}, f32[3,1,6,128]{3,2,1,0:T(8,128)S(1)}, u32[]{:S(2)}, u32[]{:S(2)}) collective-permute-start(f32[3,1,6,128]{3,2,1,0:T(8,128)S(1)} %get-tuple-element.216), channel_id=1, source_target_pairs={{0,1},{1,2},{2,3},{4,5},{5,6},{6,7},{8,9},{9,10},{10,11},{12,13},{... | collective-permute-start | bytes 27656 | tf_op jit(solution)/shard_map/ppermute | solution.py:17
  15.2 5.0 %collective-permute-start.4 = (f32[3,1,6,128]{3,2,1,0:T(8,128)S(1)}, f32[3,1,6,128]{3,2,1,0:T(8,128)S(1)}, u32[]{:S(2)}, u32[]{:S(2)}) collective-permute-start(f32[3,1,6,128]{3,2,1,0:T(8,128)S(1)} %get-tuple-element.217), channel_id=1, source_target_pairs={{1,0},{2,1},{3,2},{5,4},{6,5},{7,6},{9,8},{10,9},{11,10},{13,12},{... | collective-permute-start | bytes 27656 | tf_op jit(solution)/shard_map/ppermute | solution.py:20
  23.2 153.5 %copy-start.3 = (f32[1,4,4,128,128]{4,3,2,1,0:T(8,128)S(1)}, f32[1,4,4,128,128]{4,3,2,1,0:T(8,128)}, u32[]{:S(2)}) copy-start(f32[1,4,4,128,128]{4,3,2,1,0:T(8,128)} %param.13) | copy-start | bytes 3145732
  31.7 7.0 %collective-permute-start = (f32[32,6,128]{2,1,0:T(8,128)}, f32[32,6,128]{2,1,0:T(8,128)S(1)}, u32[]{:S(2)}, u32[]{:S(2)}) collective-permute-start(f32[32,6,128]{2,1,0:T(8,128)} %pad_maximum_fusion.17), channel_id=1, source_target_pairs={{0,4},{4,8},{8,12},{12,16},{16,20},{20,24},{24,28},{1,5},{5,9},{9,... | collective-permute-start | bytes 294920 | tf_op jit(solution)/shard_map/while/body/eval_jaxpr/ppermute | solution.py:28
  48.1 7.0 %collective-permute-start = (f32[32,6,128]{2,1,0:T(8,128)}, f32[32,6,128]{2,1,0:T(8,128)S(1)}, u32[]{:S(2)}, u32[]{:S(2)}) collective-permute-start(f32[32,6,128]{2,1,0:T(8,128)} %pad_maximum_fusion.17), channel_id=1, source_target_pairs={{0,4},{4,8},{8,12},{12,16},{16,20},{20,24},{24,28},{1,5},{5,9},{9,... | collective-permute-start | bytes 294920 | tf_op jit(solution)/shard_map/while/body/eval_jaxpr/ppermute | solution.py:28
  64.6 7.1 %collective-permute-start = (f32[32,6,128]{2,1,0:T(8,128)}, f32[32,6,128]{2,1,0:T(8,128)S(1)}, u32[]{:S(2)}, u32[]{:S(2)}) collective-permute-start(f32[32,6,128]{2,1,0:T(8,128)} %pad_maximum_fusion.17), channel_id=1, source_target_pairs={{0,4},{4,8},{8,12},{12,16},{16,20},{20,24},{24,28},{1,5},{5,9},{9,... | collective-permute-start | bytes 294920 | tf_op jit(solution)/shard_map/while/body/eval_jaxpr/ppermute | solution.py:28
  81.1 7.9 %collective-permute-start = (f32[32,6,128]{2,1,0:T(8,128)}, f32[32,6,128]{2,1,0:T(8,128)S(1)}, u32[]{:S(2)}, u32[]{:S(2)}) collective-permute-start(f32[32,6,128]{2,1,0:T(8,128)} %pad_maximum_fusion.17), channel_id=1, source_target_pairs={{0,4},{4,8},{8,12},{12,16},{16,20},{20,24},{24,28},{1,5},{5,9},{9,... | collective-permute-start | bytes 294920 | tf_op jit(solution)/shard_map/while/body/eval_jaxpr/ppermute | solution.py:28
  98.5 7.9 %collective-permute-start = (f32[32,6,128]{2,1,0:T(8,128)}, f32[32,6,128]{2,1,0:T(8,128)S(1)}, u32[]{:S(2)}, u32[]{:S(2)}) collective-permute-start(f32[32,6,128]{2,1,0:T(8,128)} %pad_maximum_fusion.17), channel_id=1, source_target_pairs={{0,4},{4,8},{8,12},{12,16},{16,20},{20,24},{24,28},{1,5},{5,9},{9,... | collective-permute-start | bytes 294920 | tf_op jit(solution)/shard_map/while/body/eval_jaxpr/ppermute | solution.py:28
  115.9 7.9 %collective-permute-start = (f32[32,6,128]{2,1,0:T(8,128)}, f32[32,6,128]{2,1,0:T(8,128)S(1)}, u32[]{:S(2)}, u32[]{:S(2)}) collective-permute-start(f32[32,6,128]{2,1,0:T(8,128)} %pad_maximum_fusion.17), channel_id=1, source_target_pairs={{0,4},{4,8},{8,12},{12,16},{16,20},{20,24},{24,28},{1,5},{5,9},{9,... | collective-permute-start | bytes 294920 | tf_op jit(solution)/shard_map/while/body/eval_jaxpr/ppermute | solution.py:28
  133.3 7.9 %collective-permute-start = (f32[32,6,128]{2,1,0:T(8,128)}, f32[32,6,128]{2,1,0:T(8,128)S(1)}, u32[]{:S(2)}, u32[]{:S(2)}) collective-permute-start(f32[32,6,128]{2,1,0:T(8,128)} %pad_maximum_fusion.17), channel_id=1, source_target_pairs={{0,4},{4,8},{8,12},{12,16},{16,20},{20,24},{24,28},{1,5},{5,9},{9,... | collective-permute-start | bytes 294920 | tf_op jit(solution)/shard_map/while/body/eval_jaxpr/ppermute | solution.py:28
  150.6 7.9 %collective-permute-start = (f32[32,6,128]{2,1,0:T(8,128)}, f32[32,6,128]{2,1,0:T(8,128)S(1)}, u32[]{:S(2)}, u32[]{:S(2)}) collective-permute-start(f32[32,6,128]{2,1,0:T(8,128)} %pad_maximum_fusion.17), channel_id=1, source_target_pairs={{0,4},{4,8},{8,12},{12,16},{16,20},{20,24},{24,28},{1,5},{5,9},{9,... | collective-permute-start | bytes 294920 | tf_op jit(solution)/shard_map/while/body/eval_jaxpr/ppermute | solution.py:28
  158.6 8.0 %collective-permute-start.5 = (f32[1,4,6,128]{3,2,1,0:T(8,128)S(1)}, f32[1,4,6,128]{3,2,1,0:T(8,128)S(1)}, u32[]{:S(2)}, u32[]{:S(2)}) collective-permute-start(f32[1,4,6,128]{3,2,1,0:T(8,128)S(1)} %bitcast.102), channel_id=1, source_target_pairs={{0,4},{4,8},{8,12},{12,16},{16,20},{20,24},{24,28},{1,5},{5,9},{9,... | collective-permute-start | bytes 36872 | tf_op jit(solution)/shard_map/ppermute | solution.py:17
  163.5 5.4 %collective-permute-start.6 = (f32[1,4,6,128]{3,2,1,0:T(8,128)S(1)}, f32[1,4,6,128]{3,2,1,0:T(8,128)S(1)}, u32[]{:S(2)}, u32[]{:S(2)}) collective-permute-start(f32[1,4,6,128]{3,2,1,0:T(8,128)S(1)} %bitcast.103), channel_id=1, source_target_pairs={{4,0},{8,4},{12,8},{16,12},{20,16},{24,20},{28,24},{5,1},{9,5},{13... | collective-permute-start | bytes 36872 | tf_op jit(solution)/shard_map/ppermute | solution.py:20
  168.8 8.4 %collective-permute-start.7 = (f32[3,1,6,128]{3,2,1,0:T(8,128)S(1)}, f32[3,1,6,128]{3,2,1,0:T(8,128)S(1)}, u32[]{:S(2)}, u32[]{:S(2)}) collective-permute-start(f32[3,1,6,128]{3,2,1,0:T(8,128)S(1)} %get-tuple-element.214), channel_id=1, source_target_pairs={{0,1},{1,2},{2,3},{4,5},{5,6},{6,7},{8,9},{9,10},{10,11},{12,13},{... | collective-permute-start | bytes 27656 | tf_op jit(solution)/shard_map/ppermute | solution.py:17
  174.8 5.0 %collective-permute-start.8 = (f32[3,1,6,128]{3,2,1,0:T(8,128)S(1)}, f32[3,1,6,128]{3,2,1,0:T(8,128)S(1)}, u32[]{:S(2)}, u32[]{:S(2)}) collective-permute-start(f32[3,1,6,128]{3,2,1,0:T(8,128)S(1)} %get-tuple-element.215), channel_id=1, source_target_pairs={{1,0},{2,1},{3,2},{5,4},{6,5},{7,6},{9,8},{10,9},{11,10},{13,12},{... | collective-permute-start | bytes 27656 | tf_op jit(solution)/shard_map/ppermute | solution.py:20
where the time goes:
time: 182 us; the launch traced here: 181 us
  starting transfers between devices  60.8 us (33%)
  blocking collectives  47.4 us (26%)
  waiting for transfers between devices  32.6 us (18%)
  matrix products  25.2 us (14%)
  local copies, waits for them, and re-layouts  8.22 us (5%)
  other arithmetic  6.17 us (3%)
    all_gather x8, blocking collectives, advance(): whole = lax.all_gather(solved, 'face', axis=0, tiled=True)  47.4 us
    ppermute x8, starting transfers between devices, passed_along(): return lax.ppermute(block, axis, route)  33.9 us
    ppermute x8, waiting for transfers between devices, passed_along(): return lax.ppermute(block, axis, route)  26.8 us
    ppermute x4, starting transfers between devices, padded_2(): lax.ppermute(lax.slice_in_dim(block, block.shape[dim] - width, None, axis...  19.1 us
    dot_general x8, matrix products, fill_term(): jnp.einsum('rkij,rklj->rli', blocks, picked * inside[:, :, None, None], p...  11.3 us
    dot_general x10, matrix products, apply_blocks(): jnp.einsum('srij,srlj->srli', mats, vecs, precision=lax.Precision.HIGHEST)  9.66 us
    ppermute x4, starting transfers between devices, padded_2(): lax.ppermute(lax.slice_in_dim(block, 0, width, axis=dim), axis, backward)  7.89 us
    ppermute x4, waiting for transfers between devices, padded_2(): lax.ppermute(lax.slice_in_dim(block, 0, width, axis=dim), axis, backward)  5.78 us
  transfers between devices with their start and end apart: 16, of which 12 were waited for; matrix products, arithmetic and copies ran while one was open for 4% of the time, Pallas kernels for 0%

commit v1 on v0

v1 whole, which is shorter than its diff:
```python
import functools

import jax
import jax.numpy as jnp
from jax import lax
from jax.experimental import pallas as pl
from jax.experimental.pallas import tpu as pltpu
from jax.sharding import PartitionSpec as P

MESH = pl.DeviceIdType.MESH
NT = (((1,), (1,)), ((), ()))
F32, BF16 = jnp.float32, jnp.bfloat16


def halves(x):
    high = x.astype(BF16)
    return high, (x - high.astype(F32)).astype(BF16)


def rows_of(v):
    high = v.astype(BF16).astype(F32)
    return jnp.concatenate([high, v - high], axis=0).astype(BF16)


def product(x, w):
    y = lax.dot_general(x, w, NT, preferred_element_type=F32)
    n = w.shape[0] // 2
    return y[:8, :n] + (y[:8, n:] + y[8:, :n])


def kernel(
    dims,
    rhs, it, ops, opc, slot, cnt, fill, dinv,
    sol_out, img_out,
    v_rhs, v_it, v_ops, v_opc, v_fill, v_dinv,
    it_prev, it_next, it_lo, it_hi,
    w_op, w_fill, w_inv,
    part, sol, v_sol, v_img, win1, win2, s_next, s_lo, s_hi,
    load_sem, out_sem, it_send, it_recv, one_send, one_recv, two_send, two_recv, near_send, near_recv,
):
    slabs, faces, rows, loads, blk, fills = dims
    s, f = lax.axis_index("slab"), lax.axis_index("face")
    own = rows * loads
    slab_rows = faces * rows
    has_prev, has_next = s > 0, s < slabs - 1
    has_lo, has_hi = f > 0, f < faces - 1

    pairs = ((it, v_it), (rhs, v_rhs), (ops, v_ops), (opc, v_opc), (dinv, v_dinv), (fill, v_fill))
    loading = [
        pltpu.make_async_copy(a.at[0], b, load_sem.at[n]) for n, (a, b) in enumerate(pairs)
    ]
    for c in loading:
        c.start()

    barrier = pltpu.get_barrier_semaphore()

    def greet(ok, who):
        @pl.when(ok)
        def _():
            pl.semaphore_signal(barrier, inc=1, device_id=who, device_id_type=MESH)

    greet(has_next, (s + 1, f))
    greet(has_lo, (s, f - 1))
    greet(has_hi, (s, f + 1))
    for g in range(faces):
        greet(has_prev, (s - 1, g))
    for g in range(faces):
        greet(s > 1, (s - 2, g))

    peers = has_prev.astype(jnp.int32) + has_lo.astype(jnp.int32) + has_hi.astype(jnp.int32)
    peers = peers + faces * (has_next.astype(jnp.int32) + (s < slabs - 2).astype(jnp.int32))
    pl.semaphore_wait(barrier, peers)

    def remote(src, dst, a, b, who):
        return pltpu.make_async_remote_copy(
            src_ref=src, dst_ref=dst, send_sem=a, recv_sem=b, device_id=who, device_id_type=MESH
        )

    halo = (
        (has_next, has_prev, it.at[0], it_prev, (s + 1, f)),
        (has_prev, has_next, it.at[0], it_next, (s - 1, f)),
        (has_hi, has_lo, it.at[0, pl.ds(rows - 1, 1)], it_lo, (s, f + 1)),
        (has_lo, has_hi, it.at[0, pl.ds(0, 1)], it_hi, (s, f - 1)),
    )
    halo_copies = []
    for n, (sends, gets, src, dst, who) in enumerate(halo):
        c = remote(src, dst, it_send.at[n], it_recv.at[n], who)
        halo_copies.append(c)
        pl.when(sends)(c.start)

        @pl.when(jnp.logical_not(gets))
        def _(dst=dst):
            dst[...] = jnp.zeros_like(dst)

    @pl.when(jnp.logical_not(has_prev))
    def _():
        win1[...] = jnp.zeros_like(win1)

    @pl.when(jnp.logical_not(has_next))
    def _():
        s_next[...] = jnp.zeros_like(s_next)

    @pl.when(jnp.logical_not(has_lo))
    def _():
        s_lo[...] = jnp.zeros_like(s_lo)

    @pl.when(jnp.logical_not(has_hi))
    def _():
        s_hi[...] = jnp.zeros_like(s_hi)

    for c in loading[:4]:
        c.wait()

    for r in range(rows):
        blocks = (v_ops[r], v_opc[r, 0], v_opc[r, 2], v_opc[r, 3], v_opc[r, 1])
        for n, m in enumerate(blocks):
            high, low = halves(m)
            w_op[r, :blk, n * blk : (n + 1) * blk] = high
            w_op[r, blk:, n * blk : (n + 1) * blk] = low
    loading[4].wait()
    for r in range(rows):
        high, low = halves(v_dinv[r])
        w_inv[r, :blk] = high
        w_inv[r, blk:] = low

    for c, (sends, gets, *_) in zip(halo_copies, halo):
        pl.when(gets)(c.wait_recv)

    fill_up = jnp.zeros((8 - loads, blk), F32)

    def up(v):
        return jnp.concatenate([v, fill_up], axis=0)

    for r in range(rows):
        before = it_lo[0] if r == 0 else v_it[r - 1]
        after = it_hi[0] if r == rows - 1 else v_it[r + 1]
        x = jnp.concatenate(
            [rows_of(up(v)) for v in (v_it[r], it_prev[r], before, after, it_next[r])], axis=1
        )
        residual = up(v_rhs[r]) - product(x, w_op[r])
        part[r] = product(rows_of(residual), w_inv[r])

    def to_next(g):
        return remote(
            sol, win1.at[pl.ds(f * own, own)], one_send.at[g], one_recv.at[f], (s + 1, g)
        )

    def to_second(g):
        return remote(
            sol, win2.at[pl.ds(f * own, own)], two_send.at[g], two_recv.at[f], (s + 2, g)
        )

    def arrive(win, sem, g):
        return remote(sol, win.at[pl.ds(g * own, own)], one_send.at[g], sem.at[g], (s, f))

    near = (
        (has_prev, has_next, sol, s_next, (s - 1, f)),
        (has_hi, has_lo, sol.at[pl.ds(own - 8, 8)], s_lo, (s, f + 1)),
        (has_lo, has_hi, sol.at[pl.ds(0, 8)], s_hi, (s, f - 1)),
    )
    near_copies = [
        remote(src, dst, near_send.at[n], near_recv.at[n], who)
        for n, (_, _, src, dst, who) in enumerate(near)
    ]

    def spread():
        @pl.when(has_next)
        def _():
            for g in range(faces):
                to_next(g).start()

        for c, (sends, *_) in zip(near_copies[1:], near[1:]):
            pl.when(sends)(c.start)
        pl.when(has_prev)(near_copies[0].start)

        @pl.when(s < slabs - 2)
        def _():
            for g in range(faces):
                to_second(g).start()

    @pl.when(jnp.logical_not(has_prev))
    def _():
        for r in range(rows):
            sol[r * loads : (r + 1) * loads] = part[r][:loads]
        spread()

    loading[5].wait()

    @pl.when(has_prev)
    def _():
        for r in range(rows):
            left = jnp.concatenate([w_inv[r, :blk], w_inv[r, blk:]], axis=1)
            for k in range(fills):
                high, low = halves(v_fill[r, k])
                right = jnp.concatenate(
                    [
                        jnp.concatenate([high, low], axis=1),
                        jnp.concatenate([high, jnp.zeros_like(low)], axis=1),
                    ],
                    axis=0,
                )
                y = jnp.dot(left, right, preferred_element_type=F32)
                high, low = halves(y[:, :blk] + y[:, blk:])
                w_fill[r, :blk, k * blk : (k + 1) * blk] = high
                w_fill[r, blk:, k * blk : (k + 1) * blk] = low

    def gathered(win, r, base):
        xs = []
        for k in range(fills):
            q = slot[0, r, k] - base
            ok = jnp.logical_and(jnp.logical_and(q >= 0, q < slab_rows), k < cnt[0, r])
            q = jnp.clip(q, 0, slab_rows - 1)
            v = win[pl.ds(q * loads, 8), :]
            xs.append(rows_of(jnp.where(ok, v, 0.0)))
        return jnp.concatenate(xs, axis=1)

    @pl.when(s > 1)
    def _():
        for g in range(faces):
            arrive(win2, two_recv, g).wait_recv()
        for r in range(rows):
            part[r] = part[r] - product(gathered(win2, r, 0), w_fill[r])

    @pl.when(has_prev)
    def _():
        for g in range(faces):
            arrive(win1, one_recv, g).wait_recv()
        for r in range(rows):
            y = part[r] - product(gathered(win1, r, slab_rows), w_fill[r])
            sol[r * loads : (r + 1) * loads] = y[:loads]
        spread()

    for r in range(rows):
        v_sol[r] = sol[r * loads : (r + 1) * loads]
    sol_copy = pltpu.make_async_copy(v_sol, sol_out.at[0], out_sem.at[0])
    sol_copy.start()

    def mine(ref, r):
        return rows_of(up(ref[r * loads : (r + 1) * loads]))

    for r in range(rows):
        x = jnp.concatenate(
            [
                mine(sol, r),
                rows_of(up(win1[pl.ds(f * own + r * loads, loads), :])),
            ],
            axis=1,
        )
        part[r] = product(x, w_op[r, :, : 2 * blk])
    for c, (_, gets, *_) in zip(near_copies[1:], near[1:]):
        pl.when(gets)(c.wait_recv)
    for r in range(rows):
        before = rows_of(up(s_lo[8 - loads :])) if r == 0 else mine(sol, r - 1)
        after = rows_of(up(s_hi[:loads])) if r == rows - 1 else mine(sol, r + 1)
        x = jnp.concatenate([before, after], axis=1)
        part[r] = part[r] + product(x, w_op[r, :, 2 * blk : 4 * blk])
    pl.when(has_next)(near_copies[0].wait_recv)
    for r in range(rows):
        y = part[r] + product(mine(s_next, r), w_op[r, :, 4 * blk :])
        v_img[r] = y[:loads]
    img_copy = pltpu.make_async_copy(v_img, img_out.at[0], out_sem.at[1])
    img_copy.start()

    for c, (sends, *_) in zip(halo_copies, halo):
        pl.when(sends)(c.wait_send)
    for c, (sends, *_) in zip(near_copies, near):
        pl.when(sends)(c.wait_send)

    @pl.when(has_next)
    def _():
        for g in range(faces):
            to_next(g).wait_send()

    @pl.when(s < slabs - 2)
    def _():
        for g in range(faces):
            to_second(g).wait_send()

    sol_copy.wait()
    img_copy.wait()


def body(slabs, faces, *args):
    rhs, _, ops, opc, _, _, fill, dinv = args
    _, rows, loads, blk = rhs.shape
    fills = fill.shape[2]
    own = rows * loads
    dims = (slabs, faces, rows, loads, blk, fills)
    small = (rows, loads, blk)
    anywhere = pl.BlockSpec(memory_space=pl.ANY)
    smem = pl.BlockSpec(memory_space=pltpu.SMEM)
    out = jax.ShapeDtypeStruct(rhs.shape, F32)
    dma = pltpu.SemaphoreType.DMA
    return pl.pallas_call(
        functools.partial(kernel, dims),
        out_shape=(out, out),
        in_specs=[anywhere] * 4 + [smem] * 2 + [anywhere] * 2,
        out_specs=(anywhere, anywhere),
        scratch_shapes=[
            pltpu.VMEM(small, F32),
            pltpu.VMEM(small, F32),
            pltpu.VMEM(ops.shape[1:], F32),
            pltpu.VMEM(opc.shape[1:], F32),
            pltpu.VMEM(fill.shape[1:], F32),
            pltpu.VMEM(dinv.shape[1:], F32),
            pltpu.VMEM(small, F32),
            pltpu.VMEM(small, F32),
            pltpu.VMEM((1, loads, blk), F32),
            pltpu.VMEM((1, loads, blk), F32),
            pltpu.VMEM((rows, 2 * blk, 5 * blk), BF16),
            pltpu.VMEM((rows, 2 * blk, fills * blk), BF16),
            pltpu.VMEM((rows, 2 * blk, blk), BF16),
            pltpu.VMEM((rows, 8, blk), F32),
            pltpu.VMEM((own, blk), F32),
            pltpu.VMEM(small, F32),
            pltpu.VMEM(small, F32),
            pltpu.VMEM((faces * own + 8, blk), F32),
            pltpu.VMEM((faces * own + 8, blk), F32),
            pltpu.VMEM((own, blk), F32),
            pltpu.VMEM((8, blk), F32),
            pltpu.VMEM((8, blk), F32),
            dma((6,)),
            dma((2,)),
            dma((4,)),
            dma((4,)),
            dma((faces,)),
            dma((faces,)),
            dma((faces,)),
            dma((faces,)),
            dma((3,)),
            dma((3,)),
        ],
        compiler_params=pltpu.CompilerParams(
            collective_id=0, has_side_effects=True, vmem_limit_bytes=32 * 2**20
        ),
        cost_estimate=pl.CostEstimate(
            flops=2 * rows * (2 * 5 + fills + 1) * blk * blk * loads,
            bytes_accessed=4 * rows * (6 + fills) * blk * blk,
            transcendentals=0,
        ),
    )(*args)


def solution(mesh):
    four = P("slab", "face", None, None)
    five = P("slab", "face", None, None, None)
    return jax.shard_map(
        functools.partial(body, mesh.shape["slab"], mesh.shape["face"]),
        mesh=mesh,
        in_specs=(four, four, four, five, P("slab", "face", None), P("slab", "face"), five, four),
        out_specs=(four, four),
        check_vma=False,
    )
```

time: 182 us -> 47.1 us (0.26)
  the two profiles are of different devices: /device:TPU:5 before, /device:TPU:24 now
where the time goes in v1:
time: 47.1 us; the launch traced here: 46.7 us
  Pallas kernels  37.6 us (80%)
  local copies, waits for them, and re-layouts  8.49 us (18%)
  between operations  0.64 us (1%)
    pallas_call x1, Pallas kernels, body(): pl.pallas_call(functools.partial(kernel, dims), out_shape=(out, out), in_...  37.6 us
    unnamed x14, local copies, waits for them, and re-layouts  7.28 us
    pallas_call x2, local copies, waits for them, and re-layouts, body(): pl.pallas_call(functools.partial(kernel, dims), out_shape=(out, out), in_...  1.21 us

profile of v1, /device:TPU:24, one launch (start us, length us, event | category | flops | bytes accessed | tf_op | source)
XLA Modules:
  0.0 46.7 jit_solution(13376389872396354241)
XLA Ops:
  0.6 0.7 %copy.10.rhs = f32[1,4,6,128]{3,2,1,0:T(8,128)S(1)} copy(f32[1,4,6,128]{3,1,2,0:T(4,128)} %param.8) | data formatting | bytes 24576 | tf_op args[0]
  1.3 0.7 %copy.11.it = f32[1,4,6,128]{3,2,1,0:T(8,128)S(1)} copy(f32[1,4,6,128]{3,1,2,0:T(4,128)} %param.9) | data formatting | bytes 24576 | tf_op args[1]
  2.0 0.0 copy-start
  2.0 1.4 %copy-done = f32[1,4,6,128,128]{4,3,2,1,0:T(8,128)S(1)} copy-done((f32[1,4,6,128,128]{4,3,2,1,0:T(8,128)S(1)}, f32[1,4,6,128,128]{4,3,2,1,0:T(8,128)}, u32[]{:S(2)}) %copy-start) | copy-done | bytes 1572888
  3.5 0.0 copy-start.1
  3.5 1.2 %copy-done.1 = f32[1,4,4,128,128]{4,3,2,1,0:T(8,128)S(1)} copy-done((f32[1,4,4,128,128]{4,3,2,1,0:T(8,128)S(1)}, f32[1,4,4,128,128]{4,3,2,1,0:T(8,128)}, u32[]{:S(2)}) %copy-start.1) | copy-done | bytes 1048600
  4.7 0.0 copy-start.2
  4.7 0.9 %copy-done.2 = f32[1,4,128,128]{3,2,1,0:T(8,128)S(1)} copy-done((f32[1,4,128,128]{3,2,1,0:T(8,128)S(1)}, f32[1,4,128,128]{3,2,1,0:T(8,128)}, u32[]{:S(2)}) %copy-start.2) | copy-done | bytes 262168
  5.6 0.0 copy-start.3
  5.6 0.9 %copy-done.3 = f32[1,4,128,128]{3,2,1,0:T(8,128)S(1)} copy-done((f32[1,4,128,128]{3,2,1,0:T(8,128)S(1)}, f32[1,4,128,128]{3,2,1,0:T(8,128)}, u32[]{:S(2)}) %copy-start.3) | copy-done | bytes 262168
  6.6 0.0 copy-start.4
  6.6 0.7 %copy-done.4 = s32[1,4,6]{2,1,0:T(4,128)S(1)} copy-done((s32[1,4,6]{2,1,0:T(4,128)S(1)}, s32[1,4,6]{2,1,0:T(4,128)}, u32[]{:S(2)}) %copy-start.4) | copy-done | bytes 120
  7.3 0.0 copy-start.5
  7.3 0.7 %copy-done.5 = s32[1,4]{1,0:T(1,128)S(1)} copy-done((s32[1,4]{1,0:T(1,128)S(1)}, s32[1,4]{1,0:T(1,128)}, u32[]{:S(2)}) %copy-start.5) | copy-done | bytes 40
  7.9 37.6 %shard_map.95 = (f32[1,4,6,128]{3,2,1,0:T(8,128)S(1)}, f32[1,4,6,128]{3,2,1,0:T(8,128)S(1)}) custom-call(f32[1,4,6,128]{3,2,1,0:T(8,128)S(1)} %copy.10.rhs, f32[1,4,6,128]{3,2,1,0:T(8,128)S(1)} %copy.11.it, f32[1,4,128,128]{3,2,1,0:T(8,128)S(1)} %copy-done.2, f32[1,4,4,128,128]{4,3,2,1,0:T(8,128)S(1)} %copy-done.1, s32[1,4,6]{2,1,0:T(4,128)S(1)} %copy-done.4, ...), custom_call_target="tpu_custom_call" | custom-call | flops 13369344 | bytes 3145728 | tf_op jit(solution)/shard_map/pallas_call | solution.py:294
  45.5 0.6 %copy.12 = f32[1,4,6,128]{3,1,2,0:T(4,128)} copy(f32[1,4,6,128]{3,2,1,0:T(8,128)S(1)} %get-tuple-element.2) | data formatting | bytes 24576 | tf_op jit(solution)/shard_map/pallas_call | solution.py:294
  46.1 0.6 %copy.13 = f32[1,4,6,128]{3,1,2,0:T(4,128)} copy(f32[1,4,6,128]{3,2,1,0:T(8,128)S(1)} %get-tuple-element.3) | data formatting | bytes 24576 | tf_op jit(solution)/shard_map/pallas_call | solution.py:294
Async XLA Ops:
  2.0 1.4 %copy-start = (f32[1,4,6,128,128]{4,3,2,1,0:T(8,128)S(1)}, f32[1,4,6,128,128]{4,3,2,1,0:T(8,128)}, u32[]{:S(2)}) copy-start(f32[1,4,6,128,128]{4,3,2,1,0:T(8,128)} %fill.1) | copy-start | bytes 4718596
  3.5 1.2 %copy-start.1 = (f32[1,4,4,128,128]{4,3,2,1,0:T(8,128)S(1)}, f32[1,4,4,128,128]{4,3,2,1,0:T(8,128)}, u32[]{:S(2)}) copy-start(f32[1,4,4,128,128]{4,3,2,1,0:T(8,128)} %opc.1) | copy-start | bytes 3145732
  4.7 0.9 %copy-start.2 = (f32[1,4,128,128]{3,2,1,0:T(8,128)S(1)}, f32[1,4,128,128]{3,2,1,0:T(8,128)}, u32[]{:S(2)}) copy-start(f32[1,4,128,128]{3,2,1,0:T(8,128)} %ops.1) | copy-start | bytes 786436
  5.6 0.9 %copy-start.3 = (f32[1,4,128,128]{3,2,1,0:T(8,128)S(1)}, f32[1,4,128,128]{3,2,1,0:T(8,128)}, u32[]{:S(2)}) copy-start(f32[1,4,128,128]{3,2,1,0:T(8,128)} %dinv.1) | copy-start | bytes 786436
  6.6 0.7 %copy-start.4 = (s32[1,4,6]{2,1,0:T(4,128)S(1)}, s32[1,4,6]{2,1,0:T(4,128)}, u32[]{:S(2)}) copy-start(s32[1,4,6]{2,1,0:T(4,128)} %slot.1) | copy-start | bytes 292
  7.3 0.7 %copy-start.5 = (s32[1,4]{1,0:T(1,128)S(1)}, s32[1,4]{1,0:T(1,128)}, u32[]{:S(2)}) copy-start(s32[1,4]{1,0:T(1,128)} %cnt.1) | copy-start | bytes 52

commit v2 on v1

--- a/solution.py
+++ b/solution.py
@@ -8,7 +8,6 @@
 from jax.sharding import PartitionSpec as P
 
 MESH = pl.DeviceIdType.MESH
-NT = (((1,), (1,)), ((), ()))
 F32, BF16 = jnp.float32, jnp.bfloat16
 
 
@@ -23,16 +22,16 @@
 
 
 def product(x, w):
-    y = lax.dot_general(x, w, NT, preferred_element_type=F32)
-    n = w.shape[0] // 2
+    y = jnp.dot(x, w, preferred_element_type=F32)
+    n = w.shape[1] // 2
     return y[:8, :n] + (y[:8, n:] + y[8:, :n])
 
 
 def kernel(
     dims,
-    rhs, it, ops, opc, slot, cnt, fill, dinv,
+    rhs, it, ops, opc, slot_in, cnt_in, fill, dinv,
     sol_out, img_out,
-    v_rhs, v_it, v_ops, v_opc, v_fill, v_dinv,
+    slot, cnt, v_rhs, v_it, v_ops, v_opc, v_fill, v_dinv,
     it_prev, it_next, it_lo, it_hi,
     w_op, w_fill, w_inv,
     part, sol, v_sol, v_img, win1, win2, s_next, s_lo, s_hi,
@@ -45,9 +44,12 @@
     has_prev, has_next = s > 0, s < slabs - 1
     has_lo, has_hi = f > 0, f < faces - 1
 
-    pairs = ((it, v_it), (rhs, v_rhs), (ops, v_ops), (opc, v_opc), (dinv, v_dinv), (fill, v_fill))
+    pairs = (
+        (it.at[0], v_it), (rhs.at[0], v_rhs), (ops.at[0], v_ops), (opc.at[0], v_opc),
+        (dinv.at[0], v_dinv), (fill.at[0], v_fill), (slot_in, slot), (cnt_in, cnt),
+    )
     loading = [
-        pltpu.make_async_copy(a.at[0], b, load_sem.at[n]) for n, (a, b) in enumerate(pairs)
+        pltpu.make_async_copy(a, b, load_sem.at[n]) for n, (a, b) in enumerate(pairs)
     ]
     for c in loading:
         c.start()
@@ -79,8 +81,8 @@
     halo = (
         (has_next, has_prev, it.at[0], it_prev, (s + 1, f)),
         (has_prev, has_next, it.at[0], it_next, (s - 1, f)),
-        (has_hi, has_lo, it.at[0, pl.ds(rows - 1, 1)], it_lo, (s, f + 1)),
-        (has_lo, has_hi, it.at[0, pl.ds(0, 1)], it_hi, (s, f - 1)),
+        (has_hi, has_lo, it.at[0], it_lo, (s, f + 1)),
+        (has_lo, has_hi, it.at[0], it_hi, (s, f - 1)),
     )
     halo_copies = []
     for n, (sends, gets, src, dst, who) in enumerate(halo):
@@ -114,14 +116,14 @@
     for r in range(rows):
         blocks = (v_ops[r], v_opc[r, 0], v_opc[r, 2], v_opc[r, 3], v_opc[r, 1])
         for n, m in enumerate(blocks):
-            high, low = halves(m)
-            w_op[r, :blk, n * blk : (n + 1) * blk] = high
-            w_op[r, blk:, n * blk : (n + 1) * blk] = low
+            high, low = halves(m.T)
+            w_op[r, n * blk : (n + 1) * blk, :blk] = high
+            w_op[r, n * blk : (n + 1) * blk, blk:] = low
     loading[4].wait()
     for r in range(rows):
-        high, low = halves(v_dinv[r])
-        w_inv[r, :blk] = high
-        w_inv[r, blk:] = low
+        high, low = halves(v_dinv[r].T)
+        w_inv[r, :, :blk] = high
+        w_inv[r, :, blk:] = low
 
     for c, (sends, gets, *_) in zip(halo_copies, halo):
         pl.when(gets)(c.wait_recv)
@@ -132,12 +134,12 @@
         return jnp.concatenate([v, fill_up], axis=0)
 
     for r in range(rows):
-        before = it_lo[0] if r == 0 else v_it[r - 1]
-        after = it_hi[0] if r == rows - 1 else v_it[r + 1]
+        before = it_lo[:, rows - 1] if r == 0 else v_it[:, r - 1]
+        after = it_hi[:, 0] if r == rows - 1 else v_it[:, r + 1]
         x = jnp.concatenate(
-            [rows_of(up(v)) for v in (v_it[r], it_prev[r], before, after, it_next[r])], axis=1
-        )
-        residual = up(v_rhs[r]) - product(x, w_op[r])
+            [rows_of(up(v)) for v in (v_it[:, r], it_prev[:, r], before, after, it_next[:, r])], axis=1
+        )
+        residual = up(v_rhs[:, r]) - product(x, w_op[r])
         part[r] = product(rows_of(residual), w_inv[r])
 
     def to_next(g):
@@ -184,12 +186,13 @@
             sol[r * loads : (r + 1) * loads] = part[r][:loads]
         spread()
 
-    loading[5].wait()
+    for c in loading[5:]:
+        c.wait()
 
     @pl.when(has_prev)
     def _():
         for r in range(rows):
-            left = jnp.concatenate([w_inv[r, :blk], w_inv[r, blk:]], axis=1)
+            left = jnp.concatenate(halves(v_dinv[r]), axis=1)
             for k in range(fills):
                 high, low = halves(v_fill[r, k])
                 right = jnp.concatenate(
@@ -200,9 +203,9 @@
                     axis=0,
                 )
                 y = jnp.dot(left, right, preferred_element_type=F32)
-                high, low = halves(y[:, :blk] + y[:, blk:])
-                w_fill[r, :blk, k * blk : (k + 1) * blk] = high
-                w_fill[r, blk:, k * blk : (k + 1) * blk] = low
+                high, low = halves((y[:, :blk] + y[:, blk:]).T)
+                w_fill[r, k * blk : (k + 1) * blk, :blk] = high
+                w_fill[r, k * blk : (k + 1) * blk, blk:] = low
 
     def gathered(win, r, base):
         xs = []
@@ -231,7 +234,7 @@
         spread()
 
     for r in range(rows):
-        v_sol[r] = sol[r * loads : (r + 1) * loads]
+        v_sol[:, r] = sol[r * loads : (r + 1) * loads]
     sol_copy = pltpu.make_async_copy(v_sol, sol_out.at[0], out_sem.at[0])
     sol_copy.start()
 
@@ -246,18 +249,18 @@
             ],
             axis=1,
         )
-        part[r] = product(x, w_op[r, :, : 2 * blk])
+        part[r] = product(x, w_op[r, : 2 * blk])
     for c, (_, gets, *_) in zip(near_copies[1:], near[1:]):
         pl.when(gets)(c.wait_recv)
     for r in range(rows):
         before = rows_of(up(s_lo[8 - loads :])) if r == 0 else mine(sol, r - 1)
         after = rows_of(up(s_hi[:loads])) if r == rows - 1 else mine(sol, r + 1)
         x = jnp.concatenate([before, after], axis=1)
-        part[r] = part[r] + product(x, w_op[r, :, 2 * blk : 4 * blk])
+        part[r] = part[r] + product(x, w_op[r, 2 * blk : 4 * blk])
     pl.when(has_next)(near_copies[0].wait_recv)
     for r in range(rows):
-        y = part[r] + product(mine(s_next, r), w_op[r, :, 4 * blk :])
-        v_img[r] = y[:loads]
+        y = part[r] + product(mine(s_next, r), w_op[r, 4 * blk :])
+        v_img[:, r] = y[:loads]
     img_copy = pltpu.make_async_copy(v_img, img_out.at[0], out_sem.at[1])
     img_copy.start()
 
@@ -281,22 +284,23 @@
 
 
 def body(slabs, faces, *args):
-    rhs, _, ops, opc, _, _, fill, dinv = args
+    rhs, it, ops, opc, slot, cnt, fill, dinv = args
     _, rows, loads, blk = rhs.shape
     fills = fill.shape[2]
     own = rows * loads
     dims = (slabs, faces, rows, loads, blk, fills)
-    small = (rows, loads, blk)
+    small = (loads, rows, blk)
     anywhere = pl.BlockSpec(memory_space=pl.ANY)
-    smem = pl.BlockSpec(memory_space=pltpu.SMEM)
-    out = jax.ShapeDtypeStruct(rhs.shape, F32)
+    out = jax.ShapeDtypeStruct((1,) + small, F32)
     dma = pltpu.SemaphoreType.DMA
-    return pl.pallas_call(
+    outs = pl.pallas_call(
         functools.partial(kernel, dims),
         out_shape=(out, out),
-        in_specs=[anywhere] * 4 + [smem] * 2 + [anywhere] * 2,
+        in_specs=[anywhere] * 8,
         out_specs=(anywhere, anywhere),
         scratch_shapes=[
+            pltpu.SMEM(slot.shape, jnp.int32),
+            pltpu.SMEM(cnt.shape, jnp.int32),
             pltpu.VMEM(small, F32),
             pltpu.VMEM(small, F32),
             pltpu.VMEM(ops.shape[1:], F32),
@@ -305,11 +309,11 @@
             pltpu.VMEM(dinv.shape[1:], F32),
             pltpu.VMEM(small, F32),
             pltpu.VMEM(small, F32),
-            pltpu.VMEM((1, loads, blk), F32),
-            pltpu.VMEM((1, loads, blk), F32),
-            pltpu.VMEM((rows, 2 * blk, 5 * blk), BF16),
-            pltpu.VMEM((rows, 2 * blk, fills * blk), BF16),
-            pltpu.VMEM((rows, 2 * blk, blk), BF16),
+            pltpu.VMEM(small, F32),
+            pltpu.VMEM(small, F32),
+            pltpu.VMEM((rows, 5 * blk, 2 * blk), BF16),
+            pltpu.VMEM((rows, fills * blk, 2 * blk), BF16),
+            pltpu.VMEM((rows, blk, 2 * blk), BF16),
             pltpu.VMEM((rows, 8, blk), F32),
             pltpu.VMEM((own, blk), F32),
             pltpu.VMEM(small, F32),
@@ -319,7 +323,7 @@
             pltpu.VMEM((own, blk), F32),
             pltpu.VMEM((8, blk), F32),
             pltpu.VMEM((8, blk), F32),
-            dma((6,)),
+            dma((8,)),
             dma((2,)),
             dma((4,)),
             dma((4,)),
@@ -331,14 +335,15 @@
             dma((3,)),
         ],
         compiler_params=pltpu.CompilerParams(
-            collective_id=0, has_side_effects=True, vmem_limit_bytes=32 * 2**20
+            collective_id=0, has_side_effects=True, vmem_limit_bytes=60 * 2**20
         ),
         cost_estimate=pl.CostEstimate(
             flops=2 * rows * (2 * 5 + fills + 1) * blk * blk * loads,
             bytes_accessed=4 * rows * (6 + fills) * blk * blk,
             transcendentals=0,
         ),
-    )(*args)
+    )(jnp.swapaxes(rhs, 1, 2), jnp.swapaxes(it, 1, 2), ops, opc, slot, cnt, fill, dinv)
+    return tuple(jnp.swapaxes(o, 1, 2) for o in outs)
 
 
 def solution(mesh):

time: 47.1 us -> 39.6 us (0.84)
  local copies, waits for them, and re-layouts: 8.49 us -> 2.61 us
  Pallas kernels: 37.6 us -> 36 us
    unnamed x14 -> x2, local copies, waits for them, and re-layouts: 7.28 us -> 2.61 us
    pallas_call x1, Pallas kernels: 37.6 us -> 36 us  [body(): pl.pallas_call(functools.partial(kernel, dims), out_shape=(out, out), in_...]
    pallas_call x2 -> x0, local copies, waits for them, and re-layouts: 1.21 us -> none  [body(): pl.pallas_call(functools.partial(kernel, dims), out_shape=(out, out), in_...]
where the time goes in v2:
time: 39.6 us; the launch traced here: 39.3 us
  Pallas kernels  36 us (91%)
  local copies, waits for them, and re-layouts  2.61 us (7%)
  between operations  0.64 us (2%)
    pallas_call x1, Pallas kernels, body(): pl.pallas_call(functools.partial(kernel, dims), out_shape=(out, out), in_...  36 us
    unnamed x2, local copies, waits for them, and re-layouts  2.61 us

profile of v2, /device:TPU:24, one launch (start us, length us, event | category | flops | bytes accessed | tf_op | source)
XLA Modules:
  0.0 39.3 jit_solution(15903448997006686722)
XLA Ops:
  0.6 36.0 %shard_map.95 = (f32[1,6,4,128]{3,2,1,0:T(4,128)}, f32[1,6,4,128]{3,2,1,0:T(4,128)}) custom-call(f32[1,6,4,128]{3,2,1,0:T(4,128)} %bitcast.4, f32[1,6,4,128]{3,2,1,0:T(4,128)} %bitcast.5, f32[1,4,128,128]{3,2,1,0:T(8,128)} %ops.1, f32[1,4,4,128,128]{4,3,2,1,0:T(8,128)} %opc.1, s32[1,4,6]{2,1,0:T(4,128)} %slot_in.1, s32[1,4]{1,0:T(1,128)} %cnt_in.1, ...), custom_call_target="tpu_custom_call" | custom-call | flops 13369344 | bytes 3145728 | tf_op jit(solution)/shard_map/pallas_call | solution.py:296
  36.7 1.3 %copy.12 = f32[1,4,6,128]{3,1,2,0:T(4,128)} copy(f32[1,4,6,128]{3,1,2,0:T(4,128)} %bitcast.7) | data formatting | bytes 24576
  38.0 1.3 %copy.13 = f32[1,4,6,128]{3,1,2,0:T(4,128)} copy(f32[1,4,6,128]{3,1,2,0:T(4,128)} %bitcast.6) | data formatting | bytes 24576

commit v3 on v2

--- a/solution.py
+++ b/solution.py
@@ -30,12 +30,12 @@
 def kernel(
     dims,
     rhs, it, ops, opc, slot_in, cnt_in, fill, dinv,
-    sol_out, img_out,
+    out,
     slot, cnt, v_rhs, v_it, v_ops, v_opc, v_fill, v_dinv,
     it_prev, it_next, it_lo, it_hi,
     w_op, w_fill, w_inv,
-    part, sol, v_sol, v_img, win1, win2, s_next, s_lo, s_hi,
-    load_sem, out_sem, it_send, it_recv, one_send, one_recv, two_send, two_recv, near_send, near_recv,
+    part, sol, win1, win2, s_next, s_lo, s_hi,
+    load_sem, it_send, it_recv, one_send, one_recv, two_send, two_recv, near_send, near_recv,
 ):
     slabs, faces, rows, loads, blk, fills = dims
     s, f = lax.axis_index("slab"), lax.axis_index("face")
@@ -69,6 +69,15 @@
     for g in range(faces):
         greet(s > 1, (s - 2, g))
 
+    for c in loading[:4]:
+        c.wait()
+
+    for r in range(rows):
+        blocks = (v_ops[r], v_opc[r, 0], v_opc[r, 2], v_opc[r, 3], v_opc[r, 1])
+        for n, m in enumerate(blocks):
+            high, low = halves(m.T)
+            w_op[r, n * blk : (n + 1) * blk, :blk] = high
+            w_op[r, n * blk : (n + 1) * blk, blk:] = low
     peers = has_prev.astype(jnp.int32) + has_lo.astype(jnp.int32) + has_hi.astype(jnp.int32)
     peers = peers + faces * (has_next.astype(jnp.int32) + (s < slabs - 2).astype(jnp.int32))
     pl.semaphore_wait(barrier, peers)
@@ -110,15 +119,6 @@
     def _():
         s_hi[...] = jnp.zeros_like(s_hi)
 
-    for c in loading[:4]:
-        c.wait()
-
-    for r in range(rows):
-        blocks = (v_ops[r], v_opc[r, 0], v_opc[r, 2], v_opc[r, 3], v_opc[r, 1])
-        for n, m in enumerate(blocks):
-            high, low = halves(m.T)
-            w_op[r, n * blk : (n + 1) * blk, :blk] = high
-            w_op[r, n * blk : (n + 1) * blk, blk:] = low
     loading[4].wait()
     for r in range(rows):
         high, low = halves(v_dinv[r].T)
@@ -234,9 +234,7 @@
         spread()
 
     for r in range(rows):
-        v_sol[:, r] = sol[r * loads : (r + 1) * loads]
-    sol_copy = pltpu.make_async_copy(v_sol, sol_out.at[0], out_sem.at[0])
-    sol_copy.start()
+        out[0, :, r] = sol[r * loads : (r + 1) * loads]
 
     def mine(ref, r):
         return rows_of(up(ref[r * loads : (r + 1) * loads]))
@@ -260,9 +258,7 @@
     pl.when(has_next)(near_copies[0].wait_recv)
     for r in range(rows):
         y = part[r] + product(mine(s_next, r), w_op[r, 4 * blk :])
-        v_img[:, r] = y[:loads]
-    img_copy = pltpu.make_async_copy(v_img, img_out.at[0], out_sem.at[1])
-    img_copy.start()
+        out[1, :, r] = y[:loads]
 
     for c, (sends, *_) in zip(halo_copies, halo):
         pl.when(sends)(c.wait_send)
@@ -278,9 +274,6 @@
     def _():
         for g in range(faces):
             to_second(g).wait_send()
-
-    sol_copy.wait()
-    img_copy.wait()
 
 
 def body(slabs, faces, *args):
@@ -290,14 +283,13 @@
     own = rows * loads
     dims = (slabs, faces, rows, loads, blk, fills)
     small = (loads, rows, blk)
-    anywhere = pl.BlockSpec(memory_space=pl.ANY)
-    out = jax.ShapeDtypeStruct((1,) + small, F32)
+    hbm = pl.BlockSpec(memory_space=pltpu.HBM)
     dma = pltpu.SemaphoreType.DMA
     outs = pl.pallas_call(
         functools.partial(kernel, dims),
-        out_shape=(out, out),
-        in_specs=[anywhere] * 8,
-        out_specs=(anywhere, anywhere),
+        out_shape=jax.ShapeDtypeStruct((2,) + small, F32),
+        in_specs=[hbm] * 8,
+        out_specs=pl.BlockSpec(memory_space=pltpu.VMEM),
         scratch_shapes=[
             pltpu.SMEM(slot.shape, jnp.int32),
             pltpu.SMEM(cnt.shape, jnp.int32),
@@ -316,15 +308,12 @@
             pltpu.VMEM((rows, blk, 2 * blk), BF16),
             pltpu.VMEM((rows, 8, blk), F32),
             pltpu.VMEM((own, blk), F32),
-            pltpu.VMEM(small, F32),
-            pltpu.VMEM(small, F32),
             pltpu.VMEM((faces * own + 8, blk), F32),
             pltpu.VMEM((faces * own + 8, blk), F32),
             pltpu.VMEM((own, blk), F32),
             pltpu.VMEM((8, blk), F32),
             pltpu.VMEM((8, blk), F32),
             dma((8,)),
-            dma((2,)),
             dma((4,)),
             dma((4,)),
             dma((faces,)),
@@ -343,7 +332,7 @@
             transcendentals=0,
         ),
     )(jnp.swapaxes(rhs, 1, 2), jnp.swapaxes(it, 1, 2), ops, opc, slot, cnt, fill, dinv)
-    return tuple(jnp.swapaxes(o, 1, 2) for o in outs)
+    return tuple(jnp.swapaxes(outs[n : n + 1], 1, 2) for n in (0, 1))
 
 
 def solution(mesh):

time: 39.6 us -> 38.3 us (0.967)
  local copies, waits for them, and re-layouts: 2.61 us -> 1.33 us
    unnamed x2 -> x0, local copies, waits for them, and re-layouts: 2.61 us -> none
    transpose x0 -> x1, local copies, waits for them, and re-layouts: none -> 1.33 us  [body(): return tuple((jnp.swapaxes(outs[n:n + 1], 1, 2) for n in (0, 1)))]
where the time goes in v3:
time: 38.3 us; the launch traced here: 38 us
  Pallas kernels  36 us (94%)
  local copies, waits for them, and re-layouts  1.33 us (3%)
  between operations  0.64 us (2%)
    pallas_call x1, Pallas kernels, body(): pl.pallas_call(functools.partial(kernel, dims), out_shape=jax.ShapeDtypeS...  36 us
    transpose x1, local copies, waits for them, and re-layouts, body(): return tuple((jnp.swapaxes(outs[n:n + 1], 1, 2) for n in (0, 1)))  1.33 us

profile of v3, /device:TPU:24, one launch (start us, length us, event | category | flops | bytes accessed | tf_op | source)
XLA Modules:
  0.0 38.0 jit_solution(7547873965985253467)
XLA Ops:
  0.6 36.0 %shard_map.95 = f32[2,6,4,128]{3,2,1,0:T(4,128)} custom-call(f32[1,6,4,128]{3,2,1,0:T(4,128)} %bitcast.6, f32[1,6,4,128]{3,2,1,0:T(4,128)} %bitcast.7, f32[1,4,128,128]{3,2,1,0:T(8,128)} %ops.1, f32[1,4,4,128,128]{4,3,2,1,0:T(8,128)} %opc.1, s32[1,4,6]{2,1,0:T(4,128)} %slot_in.1, s32[1,4]{1,0:T(1,128)} %cnt_in.1, f32[1,4,6,128,128]{4,3,2,1,0:T(8,128)} %fill.1, ...), custom_call_target="tpu_custom_call" | custom-call | flops 13369344 | bytes 3145728 | tf_op jit(solution)/shard_map/pallas_call | solution.py:288
  36.6 1.3 %slice_bitcast_fusion = (f32[1,4,6,128]{3,1,2,0:T(4,128)}, f32[1,4,6,128]{3,1,2,0:T(4,128)}) fusion(f32[2,6,4,128]{3,2,1,0:T(4,128)} %shard_map.95), kind=kLoop, calls=%fused_computation | loop fusion | bytes 49152 | tf_op jit(solution)/shard_map/transpose | solution.py:335

commit v4 on v3

--- a/solution.py
+++ b/solution.py
@@ -88,10 +88,10 @@
         )
 
     halo = (
-        (has_next, has_prev, it.at[0], it_prev, (s + 1, f)),
-        (has_prev, has_next, it.at[0], it_next, (s - 1, f)),
-        (has_hi, has_lo, it.at[0], it_lo, (s, f + 1)),
-        (has_lo, has_hi, it.at[0], it_hi, (s, f - 1)),
+        (has_next, has_prev, v_it, it_prev, (s + 1, f)),
+        (has_prev, has_next, v_it, it_next, (s - 1, f)),
+        (has_hi, has_lo, v_it, it_lo, (s, f + 1)),
+        (has_lo, has_hi, v_it, it_hi, (s, f - 1)),
     )
     halo_copies = []
     for n, (sends, gets, src, dst, who) in enumerate(halo):
@@ -287,7 +287,7 @@
     dma = pltpu.SemaphoreType.DMA
     outs = pl.pallas_call(
         functools.partial(kernel, dims),
-        out_shape=jax.ShapeDtypeStruct((2,) + small, F32),
+        out_shape=pltpu.VMEM((2,) + small, F32),
         in_specs=[hbm] * 8,
         out_specs=pl.BlockSpec(memory_space=pltpu.VMEM),
         scratch_shapes=[

time: 38.3 us -> 36.6 us (0.956)
  Pallas kernels: 36 us -> 35.1 us
  local copies, waits for them, and re-layouts: 1.33 us -> 0.61 us
    pallas_call x1, Pallas kernels: 36 us -> 35.1 us  [body(): pl.pallas_call(functools.partial(kernel, dims), out_shape=pltpu.VMEM((2,)...]
    transpose x1, local copies, waits for them, and re-layouts: 1.33 us -> 0.61 us  [body(): return tuple((jnp.swapaxes(outs[n:n + 1], 1, 2) for n in (0, 1)))]
where the time goes in v4:
time: 36.6 us; the launch traced here: 36.4 us
  Pallas kernels  35.1 us (96%)
  between operations  0.64 us (2%)
  local copies, waits for them, and re-layouts  0.61 us (2%)
    pallas_call x1, Pallas kernels, body(): pl.pallas_call(functools.partial(kernel, dims), out_shape=pltpu.VMEM((2,)...  35.1 us

profile of v4, /device:TPU:24, one launch (start us, length us, event | category | flops | bytes accessed | tf_op | source)
XLA Modules:
  0.0 36.4 jit_solution(7530717534079969602)
XLA Ops:
  0.6 35.1 %shard_map.95 = f32[2,6,4,128]{3,2,1,0:T(4,128)S(1)} custom-call(f32[1,6,4,128]{3,2,1,0:T(4,128)} %bitcast.6, f32[1,6,4,128]{3,2,1,0:T(4,128)} %bitcast.7, f32[1,4,128,128]{3,2,1,0:T(8,128)} %ops.1, f32[1,4,4,128,128]{4,3,2,1,0:T(8,128)} %opc.1, s32[1,4,6]{2,1,0:T(4,128)} %slot_in.1, s32[1,4]{1,0:T(1,128)} %cnt_in.1, f32[1,4,6,128,128]{4,3,2,1,0:T(8,128)} %fill.1, ...), custom_call_target="tpu_custom_call" | custom-call | flops 13369344 | bytes 3145728 | tf_op jit(solution)/shard_map/pallas_call | solution.py:288
  35.8 0.6 %slice_bitcast_fusion = (f32[1,4,6,128]{3,1,2,0:T(4,128)}, f32[1,4,6,128]{3,1,2,0:T(4,128)}) fusion(f32[2,6,4,128]{3,2,1,0:T(4,128)S(1)} %shard_map.95), kind=kLoop, calls=%fused_computation | loop fusion | bytes 49152 | tf_op jit(solution)/shard_map/transpose | solution.py:335

commit v5 on v4

--- a/solution.py
+++ b/solution.py
@@ -69,15 +69,6 @@
     for g in range(faces):
         greet(s > 1, (s - 2, g))
 
-    for c in loading[:4]:
-        c.wait()
-
-    for r in range(rows):
-        blocks = (v_ops[r], v_opc[r, 0], v_opc[r, 2], v_opc[r, 3], v_opc[r, 1])
-        for n, m in enumerate(blocks):
-            high, low = halves(m.T)
-            w_op[r, n * blk : (n + 1) * blk, :blk] = high
-            w_op[r, n * blk : (n + 1) * blk, blk:] = low
     peers = has_prev.astype(jnp.int32) + has_lo.astype(jnp.int32) + has_hi.astype(jnp.int32)
     peers = peers + faces * (has_next.astype(jnp.int32) + (s < slabs - 2).astype(jnp.int32))
     pl.semaphore_wait(barrier, peers)
@@ -86,6 +77,8 @@
         return pltpu.make_async_remote_copy(
             src_ref=src, dst_ref=dst, send_sem=a, recv_sem=b, device_id=who, device_id_type=MESH
         )
+
+    loading[0].wait()
 
     halo = (
         (has_next, has_prev, v_it, it_prev, (s + 1, f)),
@@ -119,6 +112,15 @@
     def _():
         s_hi[...] = jnp.zeros_like(s_hi)
 
+    for c in loading[1:4]:
+        c.wait()
+
+    for r in range(rows):
+        blocks = (v_ops[r], v_opc[r, 0], v_opc[r, 2], v_opc[r, 3], v_opc[r, 1])
+        for n, m in enumerate(blocks):
+            high, low = halves(m.T)
+            w_op[r, n * blk : (n + 1) * blk, :blk] = high
+            w_op[r, n * blk : (n + 1) * blk, blk:] = low
     loading[4].wait()
     for r in range(rows):
         high, low = halves(v_dinv[r].T)
@@ -239,22 +241,22 @@
     def mine(ref, r):
         return rows_of(up(ref[r * loads : (r + 1) * loads]))
 
-    for r in range(rows):
-        x = jnp.concatenate(
-            [
-                mine(sol, r),
-                rows_of(up(win1[pl.ds(f * own + r * loads, loads), :])),
-            ],
-            axis=1,
-        )
-        part[r] = product(x, w_op[r, : 2 * blk])
+    def beside(r, n):
+        return w_op[r, n * blk : (n + 1) * blk]
+
+    for r in range(rows):
+        earlier = rows_of(up(win1[pl.ds(f * own + r * loads, loads), :]))
+        y = product(jnp.concatenate([mine(sol, r), earlier], axis=1), w_op[r, : 2 * blk])
+        if r > 0:
+            y = y + product(mine(sol, r - 1), beside(r, 2))
+        if r < rows - 1:
+            y = y + product(mine(sol, r + 1), beside(r, 3))
+        part[r] = y
     for c, (_, gets, *_) in zip(near_copies[1:], near[1:]):
         pl.when(gets)(c.wait_recv)
-    for r in range(rows):
-        before = rows_of(up(s_lo[8 - loads :])) if r == 0 else mine(sol, r - 1)
-        after = rows_of(up(s_hi[:loads])) if r == rows - 1 else mine(sol, r + 1)
-        x = jnp.concatenate([before, after], axis=1)
-        part[r] = part[r] + product(x, w_op[r, 2 * blk : 4 * blk])
+    part[0] = part[0] + product(rows_of(up(s_lo[8 - loads :])), beside(0, 2))
+    last = rows - 1
+    part[last] = part[last] + product(rows_of(up(s_hi[:loads])), beside(last, 3))
     pl.when(has_next)(near_copies[0].wait_recv)
     for r in range(rows):
         y = part[r] + product(mine(s_next, r), w_op[r, 4 * blk :])

time: 36.6 us -> 36.6 us (level)
  no operation moved by 1% of the time
where the time goes in v5:
time: 36.6 us; the launch traced here: 36.4 us
  Pallas kernels  35.2 us (96%)
  between operations  0.64 us (2%)
  local copies, waits for them, and re-layouts  0.61 us (2%)
    pallas_call x1, Pallas kernels, body(): pl.pallas_call(functools.partial(kernel, dims), out_shape=pltpu.VMEM((2,)...  35.2 us

profile of v5, /device:TPU:24, one launch (start us, length us, event | category | flops | bytes accessed | tf_op | source)
XLA Modules:
  0.0 36.4 jit_solution(6545311784007685112)
XLA Ops:
  0.6 35.2 %shard_map.95 = f32[2,6,4,128]{3,2,1,0:T(4,128)S(1)} custom-call(f32[1,6,4,128]{3,2,1,0:T(4,128)} %bitcast.6, f32[1,6,4,128]{3,2,1,0:T(4,128)} %bitcast.7, f32[1,4,128,128]{3,2,1,0:T(8,128)} %ops.1, f32[1,4,4,128,128]{4,3,2,1,0:T(8,128)} %opc.1, s32[1,4,6]{2,1,0:T(4,128)} %slot_in.1, s32[1,4]{1,0:T(1,128)} %cnt_in.1, f32[1,4,6,128,128]{4,3,2,1,0:T(8,128)} %fill.1, ...), custom_call_target="tpu_custom_call" | custom-call | flops 13369344 | bytes 3145728 | tf_op jit(solution)/shard_map/pallas_call | solution.py:290
  35.8 0.6 %slice_bitcast_fusion = (f32[1,4,6,128]{3,1,2,0:T(4,128)}, f32[1,4,6,128]{3,1,2,0:T(4,128)}) fusion(f32[2,6,4,128]{3,2,1,0:T(4,128)S(1)} %shard_map.95), kind=kLoop, calls=%fused_computation | loop fusion | bytes 49152 | tf_op jit(solution)/shard_map/transpose | solution.py:337

commit v6 on v5

--- a/solution.py
+++ b/solution.py
@@ -144,14 +144,17 @@
         residual = up(v_rhs[:, r]) - product(x, w_op[r])
         part[r] = product(rows_of(residual), w_inv[r])
 
-    def to_next(g):
+    def target(n):
+        return lax.rem(f + faces // 2 + n, faces)
+
+    def to_next(n):
         return remote(
-            sol, win1.at[pl.ds(f * own, own)], one_send.at[g], one_recv.at[f], (s + 1, g)
+            sol, win1.at[pl.ds(f * own, own)], one_send.at[n], one_recv.at[f], (s + 1, target(n))
         )
 
-    def to_second(g):
+    def to_second(n):
         return remote(
-            sol, win2.at[pl.ds(f * own, own)], two_send.at[g], two_recv.at[f], (s + 2, g)
+            sol, win2.at[pl.ds(f * own, own)], two_send.at[n], two_recv.at[f], (s + 2, target(n))
         )
 
     def arrive(win, sem, g):

time: 36.6 us -> 35.5 us (0.970)
  Pallas kernels: 35.2 us -> 34.1 us
    pallas_call x1, Pallas kernels: 35.2 us -> 34.1 us  [body(): pl.pallas_call(functools.partial(kernel, dims), out_shape=pltpu.VMEM((2,)...]
where the time goes in v6:
time: 35.5 us; the launch traced here: 35.3 us
  Pallas kernels  34.1 us (96%)
  between operations  0.64 us (2%)
  local copies, waits for them, and re-layouts  0.61 us (2%)
    pallas_call x1, Pallas kernels, body(): pl.pallas_call(functools.partial(kernel, dims), out_shape=pltpu.VMEM((2,)...  34.1 us

profile of v6, /device:TPU:24, one launch (start us, length us, event | category | flops | bytes accessed | tf_op | source)
XLA Modules:
  0.0 35.3 jit_solution(9920530710550888702)
XLA Ops:
  0.6 34.1 %shard_map.95 = f32[2,6,4,128]{3,2,1,0:T(4,128)S(1)} custom-call(f32[1,6,4,128]{3,2,1,0:T(4,128)} %bitcast.6, f32[1,6,4,128]{3,2,1,0:T(4,128)} %bitcast.7, f32[1,4,128,128]{3,2,1,0:T(8,128)} %ops.1, f32[1,4,4,128,128]{4,3,2,1,0:T(8,128)} %opc.1, s32[1,4,6]{2,1,0:T(4,128)} %slot_in.1, s32[1,4]{1,0:T(1,128)} %cnt_in.1, f32[1,4,6,128,128]{4,3,2,1,0:T(8,128)} %fill.1, ...), custom_call_target="tpu_custom_call" | custom-call | flops 13369344 | bytes 3145728 | tf_op jit(solution)/shard_map/pallas_call | solution.py:293
  34.7 0.6 %slice_bitcast_fusion = (f32[1,4,6,128]{3,1,2,0:T(4,128)}, f32[1,4,6,128]{3,1,2,0:T(4,128)}) fusion(f32[2,6,4,128]{3,2,1,0:T(4,128)S(1)} %shard_map.95), kind=kLoop, calls=%fused_computation | loop fusion | bytes 49152 | tf_op jit(solution)/shard_map/transpose | solution.py:340
